TPU v7x, 32 devices: a whole 2x2x4 slice. The times are simulated.
32 devices in a mesh: occ: 8 (over z, x), vir: 4 (over y, core).
Axes of the slice: x: 2, y: 2, z: 4, core: 2. Of those that a mesh axis runs over, the one named last changes fastest.
Arguments:
- amplitudes: bfloat16 [256, 16384], P('occ', 'vir'), may hold values from -6 to 6
- tile_live: int32 [8, 16], P('occ', 'vir'), may hold values from 0 to 1, as said below
- integrals: bfloat16 [16, 16, 1024, 1024], P('occ', 'vir'), may hold values from -0.046875 to 0.046875
- block_live: int32 [16, 16], P('occ', 'vir'), may hold values 0 or 1
- row_owner: int32 [16], replicated, may hold values from 0 to 15, each once
Outputs:
- residual: float32 [256, 16384], P('occ', 'vir')
Inputs may be any that keep to these rules, and one draw needn't show every extreme that they name: `tile_live`: in each pair block and each range of 4 tile pairs between 1 and 2 tiles are nonzero; some range has exactly 2. `row_owner`: each tile pair stands in exactly one slot.
All inputs are finite; a program needn't handle non-finite values. No bound on the sum of `block_live` on one device may be relied on, other than what follows from the above.
Results may differ from a plain program's by a relative error of at most 0.0003.
Values may be sent and summed in bfloat16 or wider, within the bound.
A program may use at most 128 MiB of HBM per device.

v0:
```python
import jax
import jax.numpy as jnp
from jax import lax
from jax.sharding import PartitionSpec as P


def block_term(left_rows, right_block, live_flag):
    return lax.cond(
        live_flag > 0,
        lambda: jnp.dot(left_rows, right_block, preferred_element_type=jnp.float32),
        lambda: jnp.zeros((left_rows.shape[0], right_block.shape[1]), jnp.float32),
    )


def shards(amplitudes, tile_live, integrals, block_live, row_owner):
    pair_dev = amplitudes.shape[0]
    tile_count = tile_live.shape[1]
    held_rows = integrals.shape[0]
    entry_count = integrals.shape[2]
    live_row = tile_live[0]
    masked = amplitudes.reshape(pair_dev, tile_count, entry_count) * live_row[None, :, None].astype(
        amplitudes.dtype
    )
    flattened = masked.reshape(pair_dev, tile_count * entry_count)
    row_piece = lax.all_gather(flattened, "occ", axis=0, tiled=True)
    columns = []
    for slot_index in range(held_rows):
        running = jnp.zeros((row_piece.shape[0], entry_count), jnp.float32)
        for tile_index in range(tile_count):
            offset = tile_index * entry_count
            running = running + block_term(
                row_piece[:, offset : offset + entry_count],
                integrals[slot_index, tile_index],
                block_live[slot_index, tile_index],
            )
        columns.append(running)
    partial_value = jnp.stack(columns, axis=1)
    inverse = (
        jnp.zeros(row_owner.shape, jnp.int32)
        .at[row_owner]
        .set(jnp.arange(row_owner.shape[0], dtype=jnp.int32))
    )
    exchanged = lax.all_to_all(partial_value, "occ", split_axis=0, concat_axis=1, tiled=True)
    ordered = jnp.take(exchanged, inverse, axis=1)
    summed = lax.psum_scatter(ordered, "vir", scatter_dimension=1, tiled=True)
    return summed.reshape(pair_dev, summed.shape[1] * entry_count)


def solution(mesh):
    return jax.shard_map(
        shards,
        mesh=mesh,
        in_specs=(
            P("occ", "vir"),
            P("occ", "vir"),
            P("occ", "vir", None, None),
            P("occ", "vir"),
            P(),
        ),
        out_specs=P("occ", "vir"),
        check_vma=False,
    )
```

profile of v0, /device:TPU:0, one launch (start us, length us, event | category | flops | bytes accessed | tf_op | source)
XLA Modules:
  0.0 191.7 jit_solution(16794076618722529414)
XLA Ops:
  6.5 0.0 all-gather.2.cloned.1.call-start
  6.5 0.7 convert_bitcast_fusion
  7.2 0.1 broadcast_bitcast_fusion
  7.3 1.7 broadcast_multiply_fusion
  9.0 0.0 all-gather.2.cloned.1.call-update
  9.0 1.7 fusion.27
  15.7 45.8 %all-gather.2.cloned.1.call-done = bf16[256,4096]{1,0:T(8,128)(2,1)} async-done(((bf16[32,4096]{1,0:T(8,128)(2,1)}), bf16[256,4096]{1,0:T(8,128)(2,1)}) %all-gather.2.cloned.1.call-update) | async-done | bytes 2097168 | tf_op jit(solution)/shard_map/all_gather | solution.py:25
  61.5 2.7 %fusion.26 = (bf16[256,1024]{1,0:T(8,128)(2,1)}, bf16[256,1024]{1,0:T(8,128)(2,1)S(1)}, bf16[256,1024]{1,0:T(8,128)(2,1)}, bf16[256,1024]{1,0:T(8,128)(2,1)}) fusion(bf16[256,4096]{1,0:T(8,128)(2,1)} %all-gather.2.cloned.1.call-done), kind=kLoop, calls=%fused_computation.40 | loop fusion | bytes 4194304 | tf_op jit(solution)/shard_map/slice | solution.py:32
  64.2 0.0 copy-start.1
  64.2 2.6 %conditional.10 = (f32[256,1024]{1,0:T(8,128)S(1)}) conditional(s32[]{:T(128)} %bitcast.11, () %tuple.57, (bf16[2,4,1024,1024]{3,2,1,0:T(8,128)(2,1)}, bf16[256,1024]{1,0:T(8,128)(2,1)}) %tuple.58), branch_computations={%region_5.0_spmd, %region_6.0_spmd} | conditional | flops 536870912 | bytes 3670024 | solution.py:8
  64.2 2.6 %fusion.6 = f32[256,1024]{1,0:T(8,128)S(1)} fusion(bf16[256,1024]{1,0:T(8,128)(2,1)} %get-tuple-element.81, bf16[2,4,1024,1024]{3,2,1,0:T(8,128)(2,1)} %get-tuple-element.82), kind=kOutput, calls=%fused_computation.8 | convolution fusion | flops 536870912 | bytes 3670016 | tf_op jit(solution)/shard_map/cond/branch_1_fun/dot_general | solution.py:10
  66.8 0.0 copy-done.1
  66.9 2.3 %conditional.11 = (f32[256,1024]{1,0:T(8,128)S(1)}) conditional(s32[]{:T(128)} %bitcast.12, () %tuple.59, (bf16[2,4,1024,1024]{3,2,1,0:T(8,128)(2,1)}, bf16[256,1024]{1,0:T(8,128)(2,1)S(1)}) %tuple.60), branch_computations={%region_7.0_spmd, %region_8.0_spmd} | conditional | flops 536870912 | bytes 3670024 | solution.py:8
  66.9 2.3 %fusion.9 = f32[256,1024]{1,0:T(8,128)S(1)} fusion(bf16[256,1024]{1,0:T(8,128)(2,1)S(1)} %get-tuple-element.83, bf16[2,4,1024,1024]{3,2,1,0:T(8,128)(2,1)} %get-tuple-element.84), kind=kOutput, calls=%fused_computation.11 | convolution fusion | flops 536870912 | bytes 3670016 | tf_op jit(solution)/shard_map/cond/branch_1_fun/dot_general | solution.py:10
  69.2 0.1 conditional.8
  69.2 0.1 broadcast.33
  69.3 3.5 %conditional.9 = (f32[256,1024]{1,0:T(8,128)}) conditional(s32[]{:T(128)} %bitcast.10, () %tuple.55, (bf16[2,4,1024,1024]{3,2,1,0:T(8,128)(2,1)}, bf16[256,1024]{1,0:T(8,128)(2,1)}) %tuple.56), branch_computations={%region_3.0_spmd, %region_4.0_spmd} | conditional | flops 536870912 | bytes 3670024 | solution.py:8
  69.3 3.5 %fusion.3 = f32[256,1024]{1,0:T(8,128)} fusion(bf16[256,1024]{1,0:T(8,128)(2,1)} %get-tuple-element.79, bf16[2,4,1024,1024]{3,2,1,0:T(8,128)(2,1)} %get-tuple-element.80), kind=kOutput, calls=%fused_computation.5 | convolution fusion | flops 536870912 | bytes 3670016 | tf_op jit(solution)/shard_map/cond/branch_1_fun/dot_general | solution.py:10
  72.8 1.6 add_add_fusion.1
  74.5 0.0 copy-start.3
  74.5 1.7 stack.9
  76.2 0.0 copy-done.3
  76.2 2.4 %conditional.12 = (f32[256,1024]{1,0:T(8,128)S(1)}) conditional(s32[]{:T(128)} %bitcast.13, () %tuple.61, (bf16[2,4,1024,1024]{3,2,1,0:T(8,128)(2,1)}, bf16[256,1024]{1,0:T(8,128)(2,1)S(1)}) %tuple.97), branch_computations={%region_9.0_spmd, %region_10.0_spmd} | conditional | flops 536870912 | bytes 3670024 | solution.py:8
  76.2 2.4 %fusion.12 = f32[256,1024]{1,0:T(8,128)S(1)} fusion(bf16[256,1024]{1,0:T(8,128)(2,1)S(1)} %get-tuple-element.85, bf16[2,4,1024,1024]{3,2,1,0:T(8,128)(2,1)} %get-tuple-element.86), kind=kOutput, calls=%fused_computation.14 | convolution fusion | flops 536870912 | bytes 3670016 | tf_op jit(solution)/shard_map/cond/branch_1_fun/dot_general | solution.py:10
  78.6 0.0 copy-done.2
  78.6 2.3 %conditional.13 = (f32[256,1024]{1,0:T(8,128)S(1)}) conditional(s32[]{:T(128)} %bitcast.14, () %tuple.62, (bf16[2,4,1024,1024]{3,2,1,0:T(8,128)(2,1)}, bf16[256,1024]{1,0:T(8,128)(2,1)S(1)}) %tuple.96), branch_computations={%region_11.0_spmd, %region_12.0_spmd} | conditional | flops 536870912 | bytes 3670024 | solution.py:8
  78.6 2.3 %fusion.15 = f32[256,1024]{1,0:T(8,128)S(1)} fusion(bf16[256,1024]{1,0:T(8,128)(2,1)S(1)} %get-tuple-element.87, bf16[2,4,1024,1024]{3,2,1,0:T(8,128)(2,1)} %get-tuple-element.88), kind=kOutput, calls=%fused_computation.17 | convolution fusion | flops 536870912 | bytes 3670016 | tf_op jit(solution)/shard_map/cond/branch_1_fun/dot_general | solution.py:10
  80.9 2.5 %conditional.14 = (f32[256,1024]{1,0:T(8,128)S(1)}) conditional(s32[]{:T(128)} %bitcast.15, () %tuple.63, (bf16[2,4,1024,1024]{3,2,1,0:T(8,128)(2,1)}, bf16[256,1024]{1,0:T(8,128)(2,1)}) %tuple.58), branch_computations={%region_13.0_spmd, %region_14.0_spmd} | conditional | flops 536870912 | bytes 3670024 | solution.py:8
  80.9 2.5 %fusion.18 = f32[256,1024]{1,0:T(8,128)S(1)} fusion(bf16[256,1024]{1,0:T(8,128)(2,1)} %get-tuple-element.89, bf16[2,4,1024,1024]{3,2,1,0:T(8,128)(2,1)} %get-tuple-element.90), kind=kOutput, calls=%fused_computation.20 | convolution fusion | flops 536870912 | bytes 3670016 | tf_op jit(solution)/shard_map/cond/branch_1_fun/dot_general | solution.py:10
  83.4 3.5 %conditional.15 = (f32[256,1024]{1,0:T(8,128)}) conditional(s32[]{:T(128)} %bitcast.16, () %tuple.64, (bf16[2,4,1024,1024]{3,2,1,0:T(8,128)(2,1)}, bf16[256,1024]{1,0:T(8,128)(2,1)}) %tuple.95), branch_computations={%region_15.0_spmd, %region_16.0_spmd} | conditional | flops 536870912 | bytes 3670024 | solution.py:8
  83.4 3.5 %fusion.21 = f32[256,1024]{1,0:T(8,128)} fusion(bf16[256,1024]{1,0:T(8,128)(2,1)} %get-tuple-element.91, bf16[2,4,1024,1024]{3,2,1,0:T(8,128)(2,1)} %get-tuple-element.92), kind=kOutput, calls=%fused_computation.23 | convolution fusion | flops 536870912 | bytes 3670016 | tf_op jit(solution)/shard_map/cond/branch_1_fun/dot_general | solution.py:10
  86.9 1.6 add_add_fusion
  88.5 0.0 copy-start
  88.5 0.7 stack.10
  89.3 0.5 copy-done
  89.8 3.2 %pad_maximum_fusion = f32[256,2,1024]{2,1,0:T(2,128)} fusion(f32[256,1,1024]{2,1,0:T(1,128)S(1)} %stack.10, f32[256,1,1024]{2,1,0:T(1,128)S(1)} %copy-done), kind=kLoop, calls=%fused_computation.26 | loop fusion | flops 524288 | bytes 4194304 | tf_op jit(solution)/shard_map/stack | solution.py:37
  93.0 3.7 %all-to-all-start = ((f32[256,2,1024]{2,1,0:T(2,128)}), f32[256,2,1024]{2,1,0:T(2,128)S(1)}, u32[]{:S(2)}, u32[]{:S(2)}) async-start(f32[256,2,1024]{2,1,0:T(2,128)} %pad_maximum_fusion), calls=%async_computation | async-start | bytes 4194304 | tf_op jit(solution)/shard_map/all_to_all | solution.py:43
  96.7 0.0 reduce-scatter.2.cloned.1.call-start
  96.8 0.0 copy-done.4
  96.8 0.6 scatter_custom_fusion
  97.5 49.1 %all-to-all-done = f32[256,2,1024]{2,1,0:T(2,128)S(1)} async-done(((f32[256,2,1024]{2,1,0:T(2,128)}), f32[256,2,1024]{2,1,0:T(2,128)S(1)}, u32[]{:S(2)}, u32[]{:S(2)}) %all-to-all-start) | async-done | bytes 2097184 | tf_op jit(solution)/shard_map/all_to_all | solution.py:43
  146.5 0.7 copy.8
  147.2 1.5 copy.9
  148.7 2.3 %gather_fusion = f32[16,32,1024]{2,1,0:T(8,128)S(1)} fusion(f32[32,16,1024]{2,0,1:T(8,128)} %bitcast.55, s32[1024]{0:T(1024)S(1)} %pad_clamp_fusion), kind=kCustom, calls=%fused_computation | custom fusion | bytes 4194368 | tf_op jit(solution)/shard_map/jit(_take)/gather | solution.py:44
  151.0 1.6 select_bitcast_fusion
  152.6 0.0 reduce-scatter.2.cloned.1.call-update
  152.6 30.3 %reduce-scatter.2.cloned.1.call-done = f32[32,4,1024]{2,0,1:T(8,128)} async-done(((f32[32,16,1024]{2,0,1:T(8,128)}), f32[32,4,1024]{2,0,1:T(8,128)}) %reduce-scatter.2.cloned.1.call-update) | async-done | bytes 524304 | tf_op jit(solution)/shard_map/reduce_scatter | solution.py:45
  182.9 1.9 copy.11
  (8 shorter events, 0.0 us)
Async XLA Ops:
  6.5 55.0 %all-gather.2.cloned.1.call-start = ((), (), s32[]{:S(2)}) async-start(), calls=%async_computation.2 | async-start | bytes 2359296 | tf_op jit(solution)/shard_map/all_gather | solution.py:25
  64.2 2.7 %copy-start.1 = (bf16[256,1024]{1,0:T(8,128)(2,1)}, bf16[256,1024]{1,0:T(8,128)(2,1)S(1)}, u32[]{:S(2)}) copy-start(bf16[256,1024]{1,0:T(8,128)(2,1)S(1)} %get-tuple-element.94) | copy-start | bytes 1572868
  74.5 1.7 copy-start.3
  76.2 2.4 %copy-start.2 = (bf16[256,1024]{1,0:T(8,128)(2,1)S(1)}, bf16[256,1024]{1,0:T(8,128)(2,1)}, u32[]{:S(2)}) copy-start(bf16[256,1024]{1,0:T(8,128)(2,1)} %get-tuple-element.93) | copy-start | bytes 1572868
  88.5 1.2 copy-start
  93.0 3.8 %copy-start.4 = (s32[16]{0:T(128)S(1)}, s32[16]{0:T(128)}, u32[]{:S(2)}) copy-start(s32[16]{0:T(128)} %param.25) | copy-start | bytes 196
  93.0 53.5 %all-to-all-start = ((f32[256,2,1024]{2,1,0:T(2,128)}), f32[256,2,1024]{2,1,0:T(2,128)S(1)}, u32[]{:S(2)}, u32[]{:S(2)}) async-start(f32[256,2,1024]{2,1,0:T(2,128)} %pad_maximum_fusion), calls=%async_computation | async-start | bytes 4194304 | tf_op jit(solution)/shard_map/all_to_all | solution.py:43
  96.7 86.2 %reduce-scatter.2.cloned.1.call-start = ((), (), s32[]{:S(2)}) async-start(), calls=%async_computation.3 | async-start | bytes 2621440 | tf_op jit(solution)/shard_map/reduce_scatter | solution.py:45
Sparse Core Ops, SparseCore 0:
  9.5 51.9 all-gather.1
  152.7 30.1 reduce-scatter.1
where the time goes:
time: 192 us
  waiting for transfers between devices  125 us (65%)
  matrix products  19 us (10%)
  between operations  18.6 us (10%)
  local copies, waits for them, and re-layouts  14.4 us (8%)
  other arithmetic  10.4 us (5%)
  starting transfers between devices  3.78 us (2%)
    all_to_all x1, waiting for transfers between devices, shards(): lax.all_to_all(partial_value, 'occ', split_axis=0, concat_axis=1, tiled=T...  49.1 us
    all_gather x1, waiting for transfers between devices, shards(): row_piece = lax.all_gather(flattened, 'occ', axis=0, tiled=True)  45.8 us
    reduce_scatter x1, waiting for transfers between devices, shards(): summed = lax.psum_scatter(ordered, 'vir', scatter_dimension=1, tiled=True)  30.3 us
    dot_general x7, matrix products, block_term(): jnp.dot(left_rows, right_block, preferred_element_type=jnp.float32)  19 us
  transfers between devices with their start and end apart: 3, of which 3 were waited for; matrix products, arithmetic and copies ran while one was open for 1% of the time, Pallas kernels for 0%

commit v1 on v0

v1 whole, which is shorter than its diff:
```python
import functools

import jax
import jax.numpy as jnp
from jax import lax
from jax.experimental import pallas as pl
from jax.experimental.pallas import tpu as pltpu
from jax.sharding import PartitionSpec as P

MESH = pl.DeviceIdType.MESH
LANES = 128
PACK = 2
META = 16


def kernel(
    n_occ, n_vir, amp, tile_live, block_live, row_owner, w_hbm, out,
    w, g, x, a_out, a_in, own, b_out, b_in, c_out, c_in, d_out, d_in,
    w_sem, ring_s, ring_r, pair_s, pair_r, a_s, a_r, b_s, b_r, c_s, c_r, d_s, d_r,
):
    n_u, n_y = n_occ // 2, n_vir // 2
    rows = amp.shape[0]
    slots = w_hbm.shape[0]
    tiles = tile_live.shape[1]
    entries = w_hbm.shape[2]
    np_all = row_owner.shape[0]
    out_tiles = np_all // n_vir
    cols = entries // n_vir
    pieces = entries // LANES
    f32 = jnp.float32

    occ, vir = lax.axis_index("occ"), lax.axis_index("vir")
    u, h = occ // 2, occ % 2
    y, core = vir // 2, vir % 2

    def place(o, v):
        return {"occ": o, "vir": v}

    def send(src, dst, send_sem, recv_sem, o, v):
        return pltpu.make_async_remote_copy(
            src_ref=src, dst_ref=dst, send_sem=send_sem, recv_sem=recv_sem,
            device_id=place(o, v), device_id_type=MESH,
        )

    loads = [pltpu.make_async_copy(w_hbm.at[r], w.at[r], w_sem.at[r]) for r in range(slots)]
    for load in loads:
        load.start()

    barrier = pltpu.get_barrier_semaphore()
    for d in range(1, n_occ):
        pl.semaphore_signal(barrier, inc=1, device_id=place((occ + d) % n_occ, vir), device_id_type=MESH)
    for d in range(1, n_vir):
        pl.semaphore_signal(barrier, inc=1, device_id=place(occ, (vir + d) % n_vir), device_id_type=MESH)

    live = [tile_live[0, c] for c in range(tiles)]
    chosen = []
    for k in range(PACK):
        before = 0
        line = []
        for c in range(tiles):
            line.append(jnp.where(before == k, live[c], 0).astype(f32))
            before = before + live[c]
        chosen.append(line)
    for k in range(PACK):
        for j in range(pieces):
            total = jnp.zeros((rows, LANES), f32)
            for c in range(tiles):
                at = c * entries + j * LANES
                total = total + amp[:, at : at + LANES].astype(f32) * chosen[k][c]
            g[occ, (k * pieces + j) * rows : (k * pieces + j + 1) * rows, :] = total.astype(g.dtype)
    line_index = lax.broadcasted_iota(jnp.int32, (META, LANES), 0)
    meta = jnp.zeros((META, LANES), f32)
    for k in range(PACK):
        for c in range(tiles):
            meta = meta + jnp.where(line_index == k * tiles + c, chosen[k][c], 0.0)
    g[occ, PACK * pieces * rows :, :] = meta.astype(g.dtype)

    pl.semaphore_wait(barrier, n_occ - 1 + n_vir - 1)

    def ring_copy(s):
        o = ((u + n_u - s) % n_u) * 2 + h
        return send(g.at[o], g.at[o], ring_s.at[s], ring_r.at[s], ((u + 1) % n_u) * 2 + h, vir)

    def ring_wait(s):
        o = ((u + n_u - s) % n_u) * 2 + h
        send(g.at[o], g.at[o], ring_s.at[s - 1], ring_r.at[s - 1], ((u + n_u - 1) % n_u) * 2 + h, vir).wait_recv()

    def pair_copy(s):
        o = ((u + n_u - s) % n_u) * 2 + h
        return send(g.at[o], g.at[o], pair_s.at[s], pair_r.at[s], u * 2 + 1 - h, vir)

    def pair_wait(s):
        o = ((u + n_u - s) % n_u) * 2 + 1 - h
        send(g.at[o], g.at[o], pair_s.at[s], pair_r.at[s], u * 2 + 1 - h, vir).wait_recv()

    def a_copy(s, dy):
        return send(a_out.at[s, dy], a_in.at[s, dy], a_s.at[s, dy], a_r.at[s, dy], occ, y * 2 + 1 - core)

    def b_copy(s, dy):
        return send(
            b_out.at[s, dy - 1], b_in.at[s, dy - 1], b_s.at[s, dy - 1], b_r.at[s, dy - 1],
            occ, ((y + dy) % n_y) * 2 + core,
        )

    def c_copy(s, j):
        o = ((u + n_u - s) % n_u) * 2 + (h if j == 0 else 1 - h)
        return send(
            c_out.at[s, j], c_in.at[pl.ds(occ * slots, slots)], c_s.at[s, j], c_r.at[occ], o, vir
        )

    def c_wait(d):
        o = (occ + d) % n_occ
        send(c_out.at[0, 0], c_in.at[pl.ds(o * slots, slots)], c_s.at[0, 0], c_r.at[o], o, vir).wait_recv()

    def d_copy(dv):
        return send(
            d_out.at[dv - 1], d_in.at[dv - 1], d_s.at[dv - 1], d_r.at[dv - 1], occ, (vir + dv) % n_vir
        )

    def spread(s):
        for j in range(2):
            o = ((u + n_u - s) % n_u) * 2 + (h if j == 0 else 1 - h)
            masks = g[o, PACK * pieces * rows :, :].astype(f32)
            for r in range(slots):
                for c in range(tiles):
                    flag = block_live[r, c].astype(f32)
                    m = [masks[k * tiles + c : k * tiles + c + 1, :] * flag for k in range(PACK)]
                    for i in range(pieces):
                        total = None
                        for k in range(PACK):
                            at = (k * pieces + i) * rows
                            term = g[o, at : at + rows, :].astype(f32) * m[k]
                            total = term if total is None else total + term
                        at = c * entries + i * LANES
                        x[r, j * rows : (j + 1) * rows, at : at + LANES] = total.astype(x.dtype)

    def term(r, q):
        columns = pl.ds(pl.multiple_of(q * cols, cols), cols)
        return jnp.dot(x[r], w[r, :, columns], preferred_element_type=f32)

    def finish(s):
        for dy in range(1, n_y):
            b_copy(s, dy).wait_recv()
        for j in range(2):
            at = slice(j * rows, (j + 1) * rows)
            for r in range(slots):
                total = own[s, r, at, :]
                for dy in range(1, n_y):
                    total = total + b_in[s, dy - 1, r, at, :]
                c_out[s, j, r] = total
            if j == 0:
                @pl.when(s == 0)
                def _():
                    for r in range(slots):
                        c_in[occ * slots + r] = c_out[s, j, r]

                @pl.when(s > 0)
                def _():
                    c_copy(s, j).start()
            else:
                c_copy(s, j).start()

    ring_copy(0).start()
    pair_copy(0).start()

    def step(s, carry):
        @pl.when(s + 1 < n_u)
        def _():
            ring_wait(s + 1)

            @pl.when(s + 2 < n_u)
            def _():
                ring_copy(s + 1).start()

            pair_copy(s + 1).start()

        pair_wait(s)
        spread(s)

        @pl.when(s == 0)
        def _():
            for load in loads:
                load.wait()

        for dy in list(range(1, n_y)) + [0]:
            y_to = (y + dy) % n_y
            for r in range(slots):
                a_out[s, dy, r] = term(r, y_to * 2 + 1 - core)
            a_copy(s, dy).start()
            for r in range(slots):
                mine = term(r, y_to * 2 + core)
                if dy == 0:
                    own[s, r] = mine
                else:
                    b_out[s, dy - 1, r] = mine
            a_copy(s, dy).wait_recv()
            if dy == 0:
                own[s] = own[s] + a_in[s, dy]
            else:
                b_out[s, dy - 1] = b_out[s, dy - 1] + a_in[s, dy]
                b_copy(s, dy).start()

        @pl.when(s > 0)
        def _():
            finish(s - 1)

        return carry

    lax.fori_loop(0, n_u, step, 0)
    finish(n_u - 1)

    for d in range(1, n_occ):
        c_wait(d)

    def held(p):
        slot = 0
        for r in range(np_all):
            slot = jnp.where(row_owner[r] == p, r, slot)
        return c_in[slot]

    order = [d for d in range(1, n_vir) if d % 2 == 0] + [d for d in range(1, n_vir) if d % 2]
    for dv in order:
        to = (vir + dv) % n_vir
        for t in range(out_tiles):
            d_out[dv - 1, t] = held(to * out_tiles + t)
        d_copy(dv).start()
    for t in range(out_tiles):
        at = pl.multiple_of(t * entries + vir * cols, LANES)
        out[:, pl.ds(at, cols)] = held(vir * out_tiles + t)
    for dv in order:
        d_copy(dv).wait_recv()
        q = (vir + n_vir - dv) % n_vir
        for t in range(out_tiles):
            at = pl.multiple_of(t * entries + q * cols, LANES)
            out[:, pl.ds(at, cols)] = d_in[dv - 1, t]

    for s in range(n_u):
        if s + 1 < n_u:
            ring_copy(s).wait_send()
        pair_copy(s).wait_send()
        for dy in range(n_y):
            a_copy(s, dy).wait_send()
            if dy:
                b_copy(s, dy).wait_send()
        for j in range(2):
            if s or j:
                c_copy(s, j).wait_send()
    for dv in order:
        d_copy(dv).wait_send()


def shards(n_occ, n_vir, amplitudes, tile_live, integrals, block_live, row_owner):
    rows, width = amplitudes.shape
    slots, tiles, entries, _ = integrals.shape
    np_all = row_owner.shape[0]
    n_u, n_y = n_occ // 2, n_vir // 2
    cols = entries // n_vir
    out_tiles = np_all // n_vir
    f32, bf16 = jnp.float32, jnp.bfloat16
    weights = integrals.reshape(slots, tiles * entries, entries)
    packed = PACK * (entries // LANES) * rows + META
    dma = pltpu.SemaphoreType.DMA
    vmem = pl.BlockSpec(memory_space=pltpu.VMEM)
    smem = pl.BlockSpec(memory_space=pltpu.SMEM)
    return pl.pallas_call(
        functools.partial(kernel, n_occ, n_vir),
        out_shape=jax.ShapeDtypeStruct((rows, out_tiles * entries), f32),
        in_specs=[vmem, smem, smem, smem, pl.BlockSpec(memory_space=pl.ANY)],
        out_specs=vmem,
        scratch_shapes=[
            pltpu.VMEM(weights.shape, bf16),
            pltpu.VMEM((n_occ, packed, LANES), bf16),
            pltpu.VMEM((slots, 2 * rows, tiles * entries), bf16),
            pltpu.VMEM((n_u, n_y, slots, 2 * rows, cols), f32),
            pltpu.VMEM((n_u, n_y, slots, 2 * rows, cols), f32),
            pltpu.VMEM((n_u, slots, 2 * rows, cols), f32),
            pltpu.VMEM((n_u, n_y - 1, slots, 2 * rows, cols), f32),
            pltpu.VMEM((n_u, n_y - 1, slots, 2 * rows, cols), f32),
            pltpu.VMEM((n_u, 2, slots, rows, cols), f32),
            pltpu.VMEM((np_all, rows, cols), f32),
            pltpu.VMEM((n_vir - 1, out_tiles, rows, cols), f32),
            pltpu.VMEM((n_vir - 1, out_tiles, rows, cols), f32),
            dma((slots,)),
            dma((n_u,)), dma((n_u,)), dma((n_u,)), dma((n_u,)),
            dma((n_u, n_y)), dma((n_u, n_y)),
            dma((n_u, n_y)), dma((n_u, n_y)),
            dma((n_u, 2)), dma((n_occ,)),
            dma((n_vir,)), dma((n_vir,)),
        ],
        compiler_params=pltpu.CompilerParams(
            collective_id=0, has_side_effects=True, vmem_limit_bytes=48 * 1024 * 1024
        ),
        cost_estimate=pl.CostEstimate(
            flops=2 * n_occ * rows * slots * tiles * entries * entries,
            bytes_accessed=2 * slots * tiles * entries * entries, transcendentals=0,
        ),
    )(amplitudes, tile_live, block_live, row_owner, weights)


def solution(mesh):
    n_occ, n_vir = mesh.shape["occ"], mesh.shape["vir"]
    return jax.shard_map(
        functools.partial(shards, n_occ, n_vir),
        mesh=mesh,
        in_specs=(P("occ", "vir"), P("occ", "vir"), P("occ", "vir", None, None), P("occ", "vir"), P()),
        out_specs=P("occ", "vir"),
        check_vma=False,
    )
```

time: 192 us -> 53.2 us (0.28)
  waiting for transfers between devices: 125 us -> 0 us
  Pallas kernels: 0 us -> 49.3 us
  matrix products: 19 us -> 0 us
  between operations: 18.6 us -> 0.01 us
  local copies, waits for them, and re-layouts: 14.4 us -> 3.73 us
  other arithmetic: 10.4 us -> 0 us
  starting transfers between devices: 3.78 us -> 0 us
    pallas_call x0 -> x1, Pallas kernels: none -> 49.3 us  [shards(): pl.pallas_call(functools.partial(kernel, n_occ, n_vir), out_shape=jax.Sha...]
    all_to_all x1 -> x0, waiting for transfers between devices: 49.1 us -> none  [shards(): lax.all_to_all(partial_value, 'occ', split_axis=0, concat_axis=1, tiled=T...]
    all_gather x1 -> x0, waiting for transfers between devices: 45.8 us -> none  [shards(): row_piece = lax.all_gather(flattened, 'occ', axis=0, tiled=True)]
    reduce_scatter x1 -> x0, waiting for transfers between devices: 30.3 us -> none  [shards(): summed = lax.psum_scatter(ordered, 'vir', scatter_dimension=1, tiled=True)]
    dot_general x7 -> x0, matrix products: 19 us -> none  [block_term(): jnp.dot(left_rows, right_block, preferred_element_type=jnp.float32)]
    slice x2 -> x0, local copies, waits for them, and re-layouts: 4.34 us -> none  [the longest x1 2.69 us: shards(): row_piece[:, offset:offset + entry_count]]
    all_to_all x1 -> x0, starting transfers between devices: 3.73 us -> none  [shards(): lax.all_to_all(partial_value, 'occ', split_axis=0, concat_axis=1, tiled=T...]
    add x2 -> x0, other arithmetic: 3.26 us -> none  [shards(): running + block_term(row_piece[:, offset:offset + entry_count], integrals...]
  transfers between devices with their start and end apart: 3 -> 0, of which waited for: 3 -> 0; matrix products, arithmetic and copies ran while one was open for 1% -> 0% of each run, Pallas kernels for 0% -> 0%
where the time goes in v1:
time: 53.2 us; the launch traced here: 53 us
  Pallas kernels  49.3 us (93%)
  local copies, waits for them, and re-layouts  3.73 us (7%)
    pallas_call x1, Pallas kernels, shards(): pl.pallas_call(functools.partial(kernel, n_occ, n_vir), out_shape=jax.Sha...  49.3 us
    unnamed x9, local copies, waits for them, and re-layouts  3.73 us

profile of v1, /device:TPU:0, one launch (start us, length us, event | category | flops | bytes accessed | tf_op | source)
XLA Modules:
  0.0 53.0 jit_solution(14247462269645054470)
XLA Ops:
  0.0 0.0 copy-start
  0.0 0.9 %copy-done = bf16[32,4096]{1,0:T(8,128)(2,1)S(1)} copy-done((bf16[32,4096]{1,0:T(8,128)(2,1)S(1)}, bf16[32,4096]{1,0:T(8,128)(2,1)}, u32[]{:S(2)}) %copy-start) | copy-done | bytes 262168
  1.0 0.0 copy-start.1
  1.0 0.7 %copy-done.1 = s32[2,4]{1,0:T(2,128)S(1)} copy-done((s32[2,4]{1,0:T(2,128)S(1)}, s32[2,4]{1,0:T(2,128)}, u32[]{:S(2)}) %copy-start.1) | copy-done | bytes 56
  1.6 0.0 copy-start.2
  1.6 0.7 %copy-done.2 = s32[1,4]{1,0:T(1,128)S(1)} copy-done((s32[1,4]{1,0:T(1,128)S(1)}, s32[1,4]{1,0:T(1,128)}, u32[]{:S(2)}) %copy-start.2) | copy-done | bytes 40
  2.3 0.0 copy-start.3
  2.3 0.7 %copy-done.3 = s32[16]{0:T(128)S(1)} copy-done((s32[16]{0:T(128)S(1)}, s32[16]{0:T(128)}, u32[]{:S(2)}) %copy-start.3) | copy-done | bytes 88
  2.9 49.3 %shard_map.55 = f32[32,4096]{1,0:T(8,128)S(1)} custom-call(bf16[32,4096]{1,0:T(8,128)(2,1)S(1)} %copy-done, s32[1,4]{1,0:T(1,128)S(1)} %copy-done.2, s32[2,4]{1,0:T(2,128)S(1)} %copy-done.1, s32[16]{0:T(128)S(1)} %copy-done.3, bf16[2,4096,1024]{2,1,0:T(8,128)(2,1)} %bitcast.1), custom_call_target="tpu_custom_call" | custom-call | flops 4294967296 | bytes 16777216 | tf_op jit(solution)/shard_map/pallas_call | solution.py:265
  52.2 0.8 %copy.7 = f32[32,4096]{1,0:T(8,128)} copy(f32[32,4096]{1,0:T(8,128)S(1)} %shard_map.55) | data formatting | bytes 1048576
Async XLA Ops:
  0.0 0.9 %copy-start = (bf16[32,4096]{1,0:T(8,128)(2,1)S(1)}, bf16[32,4096]{1,0:T(8,128)(2,1)}, u32[]{:S(2)}) copy-start(bf16[32,4096]{1,0:T(8,128)(2,1)} %amp.1) | copy-start | bytes 786436
  1.0 0.7 %copy-start.1 = (s32[2,4]{1,0:T(2,128)S(1)}, s32[2,4]{1,0:T(2,128)}, u32[]{:S(2)}) copy-start(s32[2,4]{1,0:T(2,128)} %block_live.1) | copy-start | bytes 100
  1.6 0.7 %copy-start.2 = (s32[1,4]{1,0:T(1,128)S(1)}, s32[1,4]{1,0:T(1,128)}, u32[]{:S(2)}) copy-start(s32[1,4]{1,0:T(1,128)} %tile_live.1) | copy-start | bytes 52
  2.3 0.7 %copy-start.3 = (s32[16]{0:T(128)S(1)}, s32[16]{0:T(128)}, u32[]{:S(2)}) copy-start(s32[16]{0:T(128)} %row_owner.1) | copy-start | bytes 196

commit v2 on v1

--- a/solution.py
+++ b/solution.py
@@ -11,11 +11,33 @@
 LANES = 128
 PACK = 2
 META = 16
+TOP = 32700.0
+FINE = 128.0
+
+
+def encode(blocks):
+    line = lax.broadcasted_iota(jnp.int32, (META, LANES), 0)
+    codes = jnp.zeros((META, LANES), jnp.float32)
+    coded = []
+    for n, block in enumerate(blocks):
+        top = jnp.maximum(jnp.max(jnp.abs(block), axis=0, keepdims=True), 1e-30)
+        code = jnp.ceil(jnp.log2(top) * FINE)
+        coded.append(jnp.round(block * (jnp.exp2(code * (-1.0 / FINE)) * TOP)).astype(jnp.int32).astype(jnp.int16))
+        codes = jnp.where(line == n, code, codes)
+    return coded, codes.astype(jnp.int32).astype(jnp.int16)
+
+
+def to_f32(value):
+    return value.astype(jnp.int32).astype(jnp.float32)
+
+
+def scales_of(codes):
+    return jnp.exp2(to_f32(codes) * (1.0 / FINE)) * (1.0 / TOP)
 
 
 def kernel(
-    n_occ, n_vir, amp, tile_live, block_live, row_owner, w_hbm, out,
-    w, g, x, a_out, a_in, own, b_out, b_in, c_out, c_in, d_out, d_in,
+    n_occ, n_vir, amp_hbm, tile_hbm, block_hbm, owner_hbm, w_hbm, out,
+    amp, tile_live, block_live, row_owner, in_sem, w, g, x, a_out, a_in, own, b_out, b_in, c_out, c_in, d_out, d_in,
     w_sem, ring_s, ring_r, pair_s, pair_r, a_s, a_r, b_s, b_r, c_s, c_r, d_s, d_r,
 ):
     n_u, n_y = n_occ // 2, n_vir // 2
@@ -42,6 +64,17 @@
             device_id=place(o, v), device_id_type=MESH,
         )
 
+    halves = cols // LANES
+    thick = rows // META
+    units = slots * halves * thick + 1
+    fetches = [
+        pltpu.make_async_copy(src, dst, in_sem.at[n])
+        for n, (src, dst) in enumerate(
+            [(amp_hbm, amp), (tile_hbm, tile_live), (block_hbm, block_live), (owner_hbm, row_owner)]
+        )
+    ]
+    for fetch in fetches:
+        fetch.start()
     loads = [pltpu.make_async_copy(w_hbm.at[r], w.at[r], w_sem.at[r]) for r in range(slots)]
     for load in loads:
         load.start()
@@ -52,6 +85,8 @@
     for d in range(1, n_vir):
         pl.semaphore_signal(barrier, inc=1, device_id=place(occ, (vir + d) % n_vir), device_id_type=MESH)
 
+    fetches[0].wait()
+    fetches[1].wait()
     live = [tile_live[0, c] for c in range(tiles)]
     chosen = []
     for k in range(PACK):
@@ -77,21 +112,28 @@
 
     pl.semaphore_wait(barrier, n_occ - 1 + n_vir - 1)
 
-    def ring_copy(s):
+    cut = pieces * rows
+    spans = [(0, cut), (cut, g.shape[1] - cut)]
+
+    def part(o, k):
+        return g.at[o, pl.ds(*spans[k])]
+
+    def ring_copy(s, k):
         o = ((u + n_u - s) % n_u) * 2 + h
-        return send(g.at[o], g.at[o], ring_s.at[s], ring_r.at[s], ((u + 1) % n_u) * 2 + h, vir)
-
-    def ring_wait(s):
+        return send(part(o, k), part(o, k), ring_s.at[s, k], ring_r.at[s, k], ((u + 1) % n_u) * 2 + h, vir)
+
+    def ring_wait(s, k):
         o = ((u + n_u - s) % n_u) * 2 + h
-        send(g.at[o], g.at[o], ring_s.at[s - 1], ring_r.at[s - 1], ((u + n_u - 1) % n_u) * 2 + h, vir).wait_recv()
-
-    def pair_copy(s):
+        left = ((u + n_u - 1) % n_u) * 2 + h
+        send(part(o, k), part(o, k), ring_s.at[s - 1, k], ring_r.at[s - 1, k], left, vir).wait_recv()
+
+    def pair_copy(s, k):
         o = ((u + n_u - s) % n_u) * 2 + h
-        return send(g.at[o], g.at[o], pair_s.at[s], pair_r.at[s], u * 2 + 1 - h, vir)
-
-    def pair_wait(s):
+        return send(part(o, k), part(o, k), pair_s.at[s, k], pair_r.at[s, k], u * 2 + 1 - h, vir)
+
+    def pair_wait(s, k):
         o = ((u + n_u - s) % n_u) * 2 + 1 - h
-        send(g.at[o], g.at[o], pair_s.at[s], pair_r.at[s], u * 2 + 1 - h, vir).wait_recv()
+        send(part(o, k), part(o, k), pair_s.at[s, k], pair_r.at[s, k], u * 2 + 1 - h, vir).wait_recv()
 
     def a_copy(s, dy):
         return send(a_out.at[s, dy], a_in.at[s, dy], a_s.at[s, dy], a_r.at[s, dy], occ, y * 2 + 1 - core)
@@ -105,16 +147,16 @@
     def c_copy(s, j):
         o = ((u + n_u - s) % n_u) * 2 + (h if j == 0 else 1 - h)
         return send(
-            c_out.at[s, j], c_in.at[pl.ds(occ * slots, slots)], c_s.at[s, j], c_r.at[occ], o, vir
+            c_out.at[s, j], c_in.at[pl.ds(occ * units, units)], c_s.at[s, j], c_r.at[occ], o, vir
         )
 
     def c_wait(d):
         o = (occ + d) % n_occ
-        send(c_out.at[0, 0], c_in.at[pl.ds(o * slots, slots)], c_s.at[0, 0], c_r.at[o], o, vir).wait_recv()
+        send(c_out.at[0, 0], c_in.at[pl.ds(o * units, units)], c_s.at[0, 0], c_r.at[o], o, vir).wait_recv()
 
     def d_copy(dv):
         return send(
-            d_out.at[dv - 1], d_in.at[dv - 1], d_s.at[dv - 1], d_r.at[dv - 1], occ, (vir + dv) % n_vir
+            d_out.at[dv], d_in.at[dv - 1], d_s.at[dv - 1], d_r.at[dv - 1], occ, (vir + dv) % n_vir
         )
 
     def spread(s):
@@ -141,18 +183,27 @@
     def finish(s):
         for dy in range(1, n_y):
             b_copy(s, dy).wait_recv()
+        scales = [scales_of(b_in[s, dy - 1, 2 * slots * halves * rows :, :]) for dy in range(1, n_y)]
         for j in range(2):
-            at = slice(j * rows, (j + 1) * rows)
+            sums = []
             for r in range(slots):
-                total = own[s, r, at, :]
-                for dy in range(1, n_y):
-                    total = total + b_in[s, dy - 1, r, at, :]
-                c_out[s, j, r] = total
+                for i in range(halves):
+                    total = own[s, r, j * rows : (j + 1) * rows, i * LANES : (i + 1) * LANES]
+                    n = (j * slots + r) * halves + i
+                    for dy in range(1, n_y):
+                        got = to_f32(b_in[s, dy - 1, n * rows : (n + 1) * rows, :])
+                        total = total + got * scales[dy - 1][n : n + 1, :]
+                    sums.append(total)
+            coded, codes = encode(sums)
+            for n, block in enumerate(coded):
+                for e in range(thick):
+                    c_out[s, j, n * thick + e] = block[e * META : (e + 1) * META, :]
+            c_out[s, j, units - 1] = codes
             if j == 0:
                 @pl.when(s == 0)
                 def _():
-                    for r in range(slots):
-                        c_in[occ * slots + r] = c_out[s, j, r]
+                    for n in range(units):
+                        c_in[occ * units + n] = c_out[s, j, n]
 
                 @pl.when(s > 0)
                 def _():
@@ -160,21 +211,26 @@
             else:
                 c_copy(s, j).start()
 
-    ring_copy(0).start()
-    pair_copy(0).start()
+    for k in range(PACK):
+        ring_copy(0, k).start()
+        pair_copy(0, k).start()
+    fetches[2].wait()
+    fetches[3].wait()
 
     def step(s, carry):
         @pl.when(s + 1 < n_u)
         def _():
-            ring_wait(s + 1)
-
-            @pl.when(s + 2 < n_u)
-            def _():
-                ring_copy(s + 1).start()
-
-            pair_copy(s + 1).start()
-
-        pair_wait(s)
+            for k in range(PACK):
+                ring_wait(s + 1, k)
+
+                @pl.when(s + 2 < n_u)
+                def _():
+                    ring_copy(s + 1, k).start()
+
+                pair_copy(s + 1, k).start()
+
+        for k in range(PACK):
+            pair_wait(s, k)
         spread(s)
 
         @pl.when(s == 0)
@@ -188,16 +244,21 @@
                 a_out[s, dy, r] = term(r, y_to * 2 + 1 - core)
             a_copy(s, dy).start()
             for r in range(slots):
-                mine = term(r, y_to * 2 + core)
-                if dy == 0:
-                    own[s, r] = mine
-                else:
-                    b_out[s, dy - 1, r] = mine
+                own[s, r] = term(r, y_to * 2 + core)
             a_copy(s, dy).wait_recv()
             if dy == 0:
                 own[s] = own[s] + a_in[s, dy]
             else:
-                b_out[s, dy - 1] = b_out[s, dy - 1] + a_in[s, dy]
+                blocks = []
+                for j in range(2):
+                    for r in range(slots):
+                        for i in range(halves):
+                            at = (r, slice(j * rows, (j + 1) * rows), slice(i * LANES, (i + 1) * LANES))
+                            blocks.append(own[(s, *at)] + a_in[(s, dy, *at)])
+                coded, codes = encode(blocks)
+                for n, block in enumerate(coded):
+                    b_out[s, dy - 1, n * rows : (n + 1) * rows, :] = block
+                b_out[s, dy - 1, 2 * slots * halves * rows :, :] = codes
                 b_copy(s, dy).start()
 
         @pl.when(s > 0)
@@ -212,32 +273,50 @@
     for d in range(1, n_occ):
         c_wait(d)
 
-    def held(p):
-        slot = 0
-        for r in range(np_all):
-            slot = jnp.where(row_owner[r] == p, r, slot)
-        return c_in[slot]
+    line = lax.broadcasted_iota(jnp.int32, (META, LANES), 0)
+
+    def stage(dv):
+        to = (vir + dv) % n_vir
+        codes = jnp.zeros((META, LANES), f32)
+        for t in range(out_tiles):
+            slot = 0
+            for r in range(np_all):
+                slot = jnp.where(row_owner[r] == to * out_tiles + t, r, slot)
+            first = (slot // slots) * units
+            lane = slot % slots
+            for n in range(halves * thick):
+                at = (t * halves * thick + n) * META
+                d_out[dv, at : at + META, :] = c_in[first + lane * (halves * thick) + n]
+            held = to_f32(c_in[first + units - 1])
+            picks = [jnp.where(lane == r, 1, 0).astype(f32) for r in range(slots)]
+            for i in range(halves):
+                code = sum(held[r * halves + i : r * halves + i + 1, :] * picks[r] for r in range(slots))
+                codes = jnp.where(line == t * halves + i, code, codes)
+        d_out[dv, out_tiles * halves * rows :, :] = codes.astype(jnp.int32).astype(jnp.int16)
+
+    def put(buf, n, q):
+        scales = scales_of(buf[n, out_tiles * halves * rows :, :])
+        for t in range(out_tiles):
+            for i in range(halves):
+                at = pl.multiple_of(t * entries + q * cols + i * LANES, LANES)
+                m = t * halves + i
+                out[:, pl.ds(at, LANES)] = to_f32(buf[n, m * rows : (m + 1) * rows, :]) * scales[m : m + 1, :]
 
     order = [d for d in range(1, n_vir) if d % 2 == 0] + [d for d in range(1, n_vir) if d % 2]
     for dv in order:
-        to = (vir + dv) % n_vir
-        for t in range(out_tiles):
-            d_out[dv - 1, t] = held(to * out_tiles + t)
+        stage(dv)
         d_copy(dv).start()
-    for t in range(out_tiles):
-        at = pl.multiple_of(t * entries + vir * cols, LANES)
-        out[:, pl.ds(at, cols)] = held(vir * out_tiles + t)
+    stage(0)
+    put(d_out, 0, vir)
     for dv in order:
         d_copy(dv).wait_recv()
-        q = (vir + n_vir - dv) % n_vir
-        for t in range(out_tiles):
-            at = pl.multiple_of(t * entries + q * cols, LANES)
-            out[:, pl.ds(at, cols)] = d_in[dv - 1, t]
+        put(d_in, dv - 1, (vir + n_vir - dv) % n_vir)
 
     for s in range(n_u):
-        if s + 1 < n_u:
-            ring_copy(s).wait_send()
-        pair_copy(s).wait_send()
+        for k in range(PACK):
+            if s + 1 < n_u:
+                ring_copy(s, k).wait_send()
+            pair_copy(s, k).wait_send()
         for dy in range(n_y):
             a_copy(s, dy).wait_send()
             if dy:
@@ -261,27 +340,36 @@
     packed = PACK * (entries // LANES) * rows + META
     dma = pltpu.SemaphoreType.DMA
     vmem = pl.BlockSpec(memory_space=pltpu.VMEM)
-    smem = pl.BlockSpec(memory_space=pltpu.SMEM)
+    i16, i32 = jnp.int16, jnp.int32
+    halves = cols // LANES
+    b_rows = 2 * slots * halves * rows + META
+    units = slots * halves * (rows // META) + 1
+    d_rows = out_tiles * halves * rows + META
     return pl.pallas_call(
         functools.partial(kernel, n_occ, n_vir),
         out_shape=jax.ShapeDtypeStruct((rows, out_tiles * entries), f32),
-        in_specs=[vmem, smem, smem, smem, pl.BlockSpec(memory_space=pl.ANY)],
+        in_specs=[pl.BlockSpec(memory_space=pltpu.HBM)] * 5,
         out_specs=vmem,
         scratch_shapes=[
+            pltpu.VMEM(amplitudes.shape, bf16),
+            pltpu.SMEM(tile_live.shape, i32),
+            pltpu.SMEM(block_live.shape, i32),
+            pltpu.SMEM(row_owner.shape, i32),
+            dma((4,)),
             pltpu.VMEM(weights.shape, bf16),
             pltpu.VMEM((n_occ, packed, LANES), bf16),
             pltpu.VMEM((slots, 2 * rows, tiles * entries), bf16),
             pltpu.VMEM((n_u, n_y, slots, 2 * rows, cols), f32),
             pltpu.VMEM((n_u, n_y, slots, 2 * rows, cols), f32),
             pltpu.VMEM((n_u, slots, 2 * rows, cols), f32),
-            pltpu.VMEM((n_u, n_y - 1, slots, 2 * rows, cols), f32),
-            pltpu.VMEM((n_u, n_y - 1, slots, 2 * rows, cols), f32),
-            pltpu.VMEM((n_u, 2, slots, rows, cols), f32),
-            pltpu.VMEM((np_all, rows, cols), f32),
-            pltpu.VMEM((n_vir - 1, out_tiles, rows, cols), f32),
-            pltpu.VMEM((n_vir - 1, out_tiles, rows, cols), f32),
+            pltpu.VMEM((n_u, n_y - 1, b_rows, LANES), i16),
+            pltpu.VMEM((n_u, n_y - 1, b_rows, LANES), i16),
+            pltpu.VMEM((n_u, 2, units, META, LANES), i16),
+            pltpu.VMEM((n_occ * units, META, LANES), i16),
+            pltpu.VMEM((n_vir, d_rows, LANES), i16),
+            pltpu.VMEM((n_vir - 1, d_rows, LANES), i16),
             dma((slots,)),
-            dma((n_u,)), dma((n_u,)), dma((n_u,)), dma((n_u,)),
+            dma((n_u, PACK)), dma((n_u, PACK)), dma((n_u, PACK)), dma((n_u, PACK)),
             dma((n_u, n_y)), dma((n_u, n_y)),
             dma((n_u, n_y)), dma((n_u, n_y)),
             dma((n_u, 2)), dma((n_occ,)),

time: 53.2 us -> 46.3 us (0.87)
  Pallas kernels: 49.3 us -> 42.3 us
    pallas_call x1, Pallas kernels: 49.3 us -> 42.3 us  [shards(): pl.pallas_call(functools.partial(kernel, n_occ, n_vir), out_shape=jax.Sha...]
where the time goes in v2:
time: 46.3 us; the launch traced here: 46 us
  Pallas kernels  42.3 us (91%)
  local copies, waits for them, and re-layouts  3.73 us (8%)
    pallas_call x1, Pallas kernels, shards(): pl.pallas_call(functools.partial(kernel, n_occ, n_vir), out_shape=jax.Sha...  42.3 us
    unnamed x9, local copies, waits for them, and re-layouts  3.73 us

profile of v2, /device:TPU:0, one launch (start us, length us, event | category | flops | bytes accessed | tf_op | source)
XLA Modules:
  0.0 46.0 jit_solution(267470134017700551)
XLA Ops:
  0.0 0.0 copy-start
  0.0 0.9 %copy-done = bf16[32,4096]{1,0:T(8,128)(2,1)S(1)} copy-done((bf16[32,4096]{1,0:T(8,128)(2,1)S(1)}, bf16[32,4096]{1,0:T(8,128)(2,1)}, u32[]{:S(2)}) %copy-start) | copy-done | bytes 262168
  1.0 0.0 copy-start.1
  1.0 0.7 %copy-done.1 = s32[2,4]{1,0:T(2,128)S(1)} copy-done((s32[2,4]{1,0:T(2,128)S(1)}, s32[2,4]{1,0:T(2,128)}, u32[]{:S(2)}) %copy-start.1) | copy-done | bytes 56
  1.6 0.0 copy-start.2
  1.6 0.7 %copy-done.2 = s32[1,4]{1,0:T(1,128)S(1)} copy-done((s32[1,4]{1,0:T(1,128)S(1)}, s32[1,4]{1,0:T(1,128)}, u32[]{:S(2)}) %copy-start.2) | copy-done | bytes 40
  2.3 0.0 copy-start.3
  2.3 0.7 %copy-done.3 = s32[16]{0:T(128)S(1)} copy-done((s32[16]{0:T(128)S(1)}, s32[16]{0:T(128)}, u32[]{:S(2)}) %copy-start.3) | copy-done | bytes 88
  2.9 42.3 %shard_map.55 = f32[32,4096]{1,0:T(8,128)S(1)} custom-call(bf16[32,4096]{1,0:T(8,128)(2,1)S(1)} %copy-done, s32[1,4]{1,0:T(1,128)S(1)} %copy-done.2, s32[2,4]{1,0:T(2,128)S(1)} %copy-done.1, s32[16]{0:T(128)S(1)} %copy-done.3, bf16[2,4096,1024]{2,1,0:T(8,128)(2,1)} %bitcast.1), custom_call_target="tpu_custom_call" | custom-call | flops 4294967296 | bytes 16777216 | tf_op jit(solution)/shard_map/pallas_call | solution.py:348
  45.2 0.8 %copy.7 = f32[32,4096]{1,0:T(8,128)} copy(f32[32,4096]{1,0:T(8,128)S(1)} %shard_map.55) | data formatting | bytes 1048576
Async XLA Ops:
  0.0 0.9 %copy-start = (bf16[32,4096]{1,0:T(8,128)(2,1)S(1)}, bf16[32,4096]{1,0:T(8,128)(2,1)}, u32[]{:S(2)}) copy-start(bf16[32,4096]{1,0:T(8,128)(2,1)} %amp_hbm.1) | copy-start | bytes 786436
  1.0 0.7 %copy-start.1 = (s32[2,4]{1,0:T(2,128)S(1)}, s32[2,4]{1,0:T(2,128)}, u32[]{:S(2)}) copy-start(s32[2,4]{1,0:T(2,128)} %block_hbm.1) | copy-start | bytes 100
  1.6 0.7 %copy-start.2 = (s32[1,4]{1,0:T(1,128)S(1)}, s32[1,4]{1,0:T(1,128)}, u32[]{:S(2)}) copy-start(s32[1,4]{1,0:T(1,128)} %tile_hbm.1) | copy-start | bytes 52
  2.3 0.7 %copy-start.3 = (s32[16]{0:T(128)S(1)}, s32[16]{0:T(128)}, u32[]{:S(2)}) copy-start(s32[16]{0:T(128)} %owner_hbm.1) | copy-start | bytes 196

commit v3 on v2

--- a/solution.py
+++ b/solution.py
@@ -9,6 +9,7 @@
 
 MESH = pl.DeviceIdType.MESH
 LANES = 128
+GROUP = 2
 PACK = 2
 META = 16
 TOP = 32700.0
@@ -41,6 +42,8 @@
     w_sem, ring_s, ring_r, pair_s, pair_r, a_s, a_r, b_s, b_r, c_s, c_r, d_s, d_r,
 ):
     n_u, n_y = n_occ // 2, n_vir // 2
+    n_g = n_u // GROUP
+    blocks_g = 2 * GROUP
     rows = amp.shape[0]
     slots = w_hbm.shape[0]
     tiles = tile_live.shape[1]
@@ -135,6 +138,9 @@
         o = ((u + n_u - s) % n_u) * 2 + 1 - h
         send(part(o, k), part(o, k), pair_s.at[s, k], pair_r.at[s, k], u * 2 + 1 - h, vir).wait_recv()
 
+    def owner(s, j):
+        return ((u + n_u - (s * GROUP + j // 2)) % n_u) * 2 + (h if j % 2 == 0 else 1 - h)
+
     def a_copy(s, dy):
         return send(a_out.at[s, dy], a_in.at[s, dy], a_s.at[s, dy], a_r.at[s, dy], occ, y * 2 + 1 - core)
 
@@ -145,7 +151,7 @@
         )
 
     def c_copy(s, j):
-        o = ((u + n_u - s) % n_u) * 2 + (h if j == 0 else 1 - h)
+        o = owner(s, j)
         return send(
             c_out.at[s, j], c_in.at[pl.ds(occ * units, units)], c_s.at[s, j], c_r.at[occ], o, vir
         )
@@ -159,9 +165,9 @@
             d_out.at[dv], d_in.at[dv - 1], d_s.at[dv - 1], d_r.at[dv - 1], occ, (vir + dv) % n_vir
         )
 
-    def spread(s):
-        for j in range(2):
-            o = ((u + n_u - s) % n_u) * 2 + (h if j == 0 else 1 - h)
+    def spread(s, step):
+        for j in range(2 * step, 2 * step + 2):
+            o = owner(s, j)
             masks = g[o, PACK * pieces * rows :, :].astype(f32)
             for r in range(slots):
                 for c in range(tiles):
@@ -183,8 +189,8 @@
     def finish(s):
         for dy in range(1, n_y):
             b_copy(s, dy).wait_recv()
-        scales = [scales_of(b_in[s, dy - 1, 2 * slots * halves * rows :, :]) for dy in range(1, n_y)]
-        for j in range(2):
+        scales = [scales_of(b_in[s, dy - 1, blocks_g * slots * halves * rows :, :]) for dy in range(1, n_y)]
+        for j in range(blocks_g):
             sums = []
             for r in range(slots):
                 for i in range(halves):
@@ -217,21 +223,34 @@
     fetches[2].wait()
     fetches[3].wait()
 
-    def step(s, carry):
-        @pl.when(s + 1 < n_u)
+    def pump(t):
+        @pl.when(t < n_u)
         def _():
             for k in range(PACK):
-                ring_wait(s + 1, k)
-
-                @pl.when(s + 2 < n_u)
+                ring_wait(t, k)
+
+                @pl.when(t + 1 < n_u)
                 def _():
-                    ring_copy(s + 1, k).start()
-
-                pair_copy(s + 1, k).start()
-
-        for k in range(PACK):
-            pair_wait(s, k)
-        spread(s)
+                    ring_copy(t, k).start()
+
+                pair_copy(t, k).start()
+
+    def step(s, carry):
+        @pl.when(s == 0)
+        def _():
+            for t in range(1, GROUP):
+                pump(t)
+
+        @pl.when(s > 0)
+        def _():
+            finish(s - 1)
+
+        for d in range(GROUP):
+            for k in range(PACK):
+                pair_wait(s * GROUP + d, k)
+            if d == GROUP - 1:
+                pump((s + 1) * GROUP)
+            spread(s, d)
 
         @pl.when(s == 0)
         def _():
@@ -250,7 +269,7 @@
                 own[s] = own[s] + a_in[s, dy]
             else:
                 blocks = []
-                for j in range(2):
+                for j in range(blocks_g):
                     for r in range(slots):
                         for i in range(halves):
                             at = (r, slice(j * rows, (j + 1) * rows), slice(i * LANES, (i + 1) * LANES))
@@ -258,17 +277,16 @@
                 coded, codes = encode(blocks)
                 for n, block in enumerate(coded):
                     b_out[s, dy - 1, n * rows : (n + 1) * rows, :] = block
-                b_out[s, dy - 1, 2 * slots * halves * rows :, :] = codes
+                b_out[s, dy - 1, blocks_g * slots * halves * rows :, :] = codes
                 b_copy(s, dy).start()
-
-        @pl.when(s > 0)
-        def _():
-            finish(s - 1)
+            if dy == n_y - 1:
+                for t in range(1, GROUP):
+                    pump((s + 1) * GROUP + t)
 
         return carry
 
-    lax.fori_loop(0, n_u, step, 0)
-    finish(n_u - 1)
+    lax.fori_loop(0, n_g, step, 0)
+    finish(n_g - 1)
 
     for d in range(1, n_occ):
         c_wait(d)
@@ -317,11 +335,12 @@
             if s + 1 < n_u:
                 ring_copy(s, k).wait_send()
             pair_copy(s, k).wait_send()
+    for s in range(n_g):
         for dy in range(n_y):
             a_copy(s, dy).wait_send()
             if dy:
                 b_copy(s, dy).wait_send()
-        for j in range(2):
+        for j in range(blocks_g):
             if s or j:
                 c_copy(s, j).wait_send()
     for dv in order:
@@ -333,6 +352,7 @@
     slots, tiles, entries, _ = integrals.shape
     np_all = row_owner.shape[0]
     n_u, n_y = n_occ // 2, n_vir // 2
+    n_g, wide = n_u // GROUP, 2 * GROUP * rows
     cols = entries // n_vir
     out_tiles = np_all // n_vir
     f32, bf16 = jnp.float32, jnp.bfloat16
@@ -342,7 +362,7 @@
     vmem = pl.BlockSpec(memory_space=pltpu.VMEM)
     i16, i32 = jnp.int16, jnp.int32
     halves = cols // LANES
-    b_rows = 2 * slots * halves * rows + META
+    b_rows = slots * halves * wide + META
     units = slots * halves * (rows // META) + 1
     d_rows = out_tiles * halves * rows + META
     return pl.pallas_call(
@@ -358,25 +378,25 @@
             dma((4,)),
             pltpu.VMEM(weights.shape, bf16),
             pltpu.VMEM((n_occ, packed, LANES), bf16),
-            pltpu.VMEM((slots, 2 * rows, tiles * entries), bf16),
-            pltpu.VMEM((n_u, n_y, slots, 2 * rows, cols), f32),
-            pltpu.VMEM((n_u, n_y, slots, 2 * rows, cols), f32),
-            pltpu.VMEM((n_u, slots, 2 * rows, cols), f32),
-            pltpu.VMEM((n_u, n_y - 1, b_rows, LANES), i16),
-            pltpu.VMEM((n_u, n_y - 1, b_rows, LANES), i16),
-            pltpu.VMEM((n_u, 2, units, META, LANES), i16),
+            pltpu.VMEM((slots, wide, tiles * entries), bf16),
+            pltpu.VMEM((n_g, n_y, slots, wide, cols), f32),
+            pltpu.VMEM((n_g, n_y, slots, wide, cols), f32),
+            pltpu.VMEM((n_g, slots, wide, cols), f32),
+            pltpu.VMEM((n_g, n_y - 1, b_rows, LANES), i16),
+            pltpu.VMEM((n_g, n_y - 1, b_rows, LANES), i16),
+            pltpu.VMEM((n_g, 2 * GROUP, units, META, LANES), i16),
             pltpu.VMEM((n_occ * units, META, LANES), i16),
             pltpu.VMEM((n_vir, d_rows, LANES), i16),
             pltpu.VMEM((n_vir - 1, d_rows, LANES), i16),
             dma((slots,)),
             dma((n_u, PACK)), dma((n_u, PACK)), dma((n_u, PACK)), dma((n_u, PACK)),
-            dma((n_u, n_y)), dma((n_u, n_y)),
-            dma((n_u, n_y)), dma((n_u, n_y)),
-            dma((n_u, 2)), dma((n_occ,)),
+            dma((n_g, n_y)), dma((n_g, n_y)),
+            dma((n_g, n_y)), dma((n_g, n_y)),
+            dma((n_g, 2 * GROUP)), dma((n_occ,)),
             dma((n_vir,)), dma((n_vir,)),
         ],
         compiler_params=pltpu.CompilerParams(
-            collective_id=0, has_side_effects=True, vmem_limit_bytes=48 * 1024 * 1024
+            collective_id=0, has_side_effects=True, vmem_limit_bytes=64 * 1024 * 1024
         ),
         cost_estimate=pl.CostEstimate(
             flops=2 * n_occ * rows * slots * tiles * entries * entries,

time: 46.3 us -> 45 us (0.972)
  local copies, waits for them, and re-layouts: 3.73 us -> 1.87 us
  Pallas kernels: 42.3 us -> 42.9 us
    unnamed x9 -> x1, local copies, waits for them, and re-layouts: 3.73 us -> 1.87 us
    pallas_call x1, Pallas kernels: 42.3 us -> 42.9 us  [shards(): pl.pallas_call(functools.partial(kernel, n_occ, n_vir), out_shape=jax.Sha...]
where the time goes in v3:
time: 45 us; the launch traced here: 44.8 us
  Pallas kernels  42.9 us (95%)
  local copies, waits for them, and re-layouts  1.87 us (4%)
    pallas_call x1, Pallas kernels, shards(): pl.pallas_call(functools.partial(kernel, n_occ, n_vir), out_shape=jax.Sha...  42.9 us
    unnamed x1, local copies, waits for them, and re-layouts  1.87 us

profile of v3, /device:TPU:0, one launch (start us, length us, event | category | flops | bytes accessed | tf_op | source)
XLA Modules:
  0.0 44.8 jit_solution(14244780627080177265)
XLA Ops:
  0.0 42.9 %shard_map.55 = f32[32,4096]{1,0:T(8,128)} custom-call(bf16[32,4096]{1,0:T(8,128)(2,1)} %amp_hbm.1, s32[1,4]{1,0:T(1,128)} %tile_hbm.1, s32[2,4]{1,0:T(2,128)} %block_hbm.1, s32[16]{0:T(128)} %owner_hbm.1, bf16[2,4096,1024]{2,1,0:T(8,128)(2,1)} %bitcast.1), custom_call_target="tpu_custom_call" | custom-call | flops 4294967296 | bytes 16777216 | tf_op jit(solution)/shard_map/pallas_call | solution.py:368
  42.9 1.9 %copy.7 = f32[32,4096]{1,0:T(8,128)} copy(f32[32,4096]{1,0:T(8,128)} %shard_map.55) | data formatting | bytes 1048576

commit v4 on v3

--- a/solution.py
+++ b/solution.py
@@ -134,6 +134,13 @@
         o = ((u + n_u - s) % n_u) * 2 + h
         return send(part(o, k), part(o, k), pair_s.at[s, k], pair_r.at[s, k], u * 2 + 1 - h, vir)
 
+    turn = n_u // 2
+
+    def relay_copy():
+        o = ((u + n_u - (turn - 1)) % n_u) * 2 + 1 - h
+        right = ((u + 1) % n_u) * 2 + h
+        return send(part(o, 1), part(o, 1), pair_s.at[turn, 1], pair_r.at[turn, 1], right, vir)
+
     def pair_wait(s, k):
         o = ((u + n_u - s) % n_u) * 2 + 1 - h
         send(part(o, k), part(o, k), pair_s.at[s, k], pair_r.at[s, k], u * 2 + 1 - h, vir).wait_recv()
@@ -144,10 +151,10 @@
     def a_copy(s, dy):
         return send(a_out.at[s, dy], a_in.at[s, dy], a_s.at[s, dy], a_r.at[s, dy], occ, y * 2 + 1 - core)
 
-    def b_copy(s, dy):
+    def b_copy(s, dy, d):
+        n = (dy - 1) * GROUP + d
         return send(
-            b_out.at[s, dy - 1], b_in.at[s, dy - 1], b_s.at[s, dy - 1], b_r.at[s, dy - 1],
-            occ, ((y + dy) % n_y) * 2 + core,
+            b_out.at[s, n], b_in.at[s, n], b_s.at[s, n], b_r.at[s, n], occ, ((y + dy) % n_y) * 2 + core
         )
 
     def c_copy(s, j):
@@ -187,18 +194,20 @@
         return jnp.dot(x[r], w[r, :, columns], preferred_element_type=f32)
 
     def finish(s):
-        for dy in range(1, n_y):
-            b_copy(s, dy).wait_recv()
-        scales = [scales_of(b_in[s, dy - 1, blocks_g * slots * halves * rows :, :]) for dy in range(1, n_y)]
         for j in range(blocks_g):
+            if j % 2 == 0:
+                for dy in range(1, n_y):
+                    b_copy(s, dy, j // 2).wait_recv()
+            from_y = [(dy - 1) * GROUP + j // 2 for dy in range(1, n_y)]
+            scales = [scales_of(b_in[s, f, 2 * slots * halves * rows :, :]) for f in from_y]
             sums = []
             for r in range(slots):
                 for i in range(halves):
                     total = own[s, r, j * rows : (j + 1) * rows, i * LANES : (i + 1) * LANES]
-                    n = (j * slots + r) * halves + i
-                    for dy in range(1, n_y):
-                        got = to_f32(b_in[s, dy - 1, n * rows : (n + 1) * rows, :])
-                        total = total + got * scales[dy - 1][n : n + 1, :]
+                    n = ((j % 2) * slots + r) * halves + i
+                    for f, scale in zip(from_y, scales):
+                        got = to_f32(b_in[s, f, n * rows : (n + 1) * rows, :])
+                        total = total + got * scale[n : n + 1, :]
                     sums.append(total)
             coded, codes = encode(sums)
             for n, block in enumerate(coded):
@@ -233,7 +242,13 @@
                 def _():
                     ring_copy(t, k).start()
 
-                pair_copy(t, k).start()
+                if k == 0:
+                    pair_copy(t, k).start()
+                else:
+
+                    @pl.when(t != turn)
+                    def _():
+                        pair_copy(t, k).start()
 
     def step(s, carry):
         @pl.when(s == 0)
@@ -248,6 +263,11 @@
         for d in range(GROUP):
             for k in range(PACK):
                 pair_wait(s * GROUP + d, k)
+
+            @pl.when(s * GROUP + d == turn - 1)
+            def _():
+                relay_copy().start()
+
             if d == GROUP - 1:
                 pump((s + 1) * GROUP)
             spread(s, d)
@@ -268,17 +288,19 @@
             if dy == 0:
                 own[s] = own[s] + a_in[s, dy]
             else:
-                blocks = []
-                for j in range(blocks_g):
-                    for r in range(slots):
-                        for i in range(halves):
-                            at = (r, slice(j * rows, (j + 1) * rows), slice(i * LANES, (i + 1) * LANES))
-                            blocks.append(own[(s, *at)] + a_in[(s, dy, *at)])
-                coded, codes = encode(blocks)
-                for n, block in enumerate(coded):
-                    b_out[s, dy - 1, n * rows : (n + 1) * rows, :] = block
-                b_out[s, dy - 1, blocks_g * slots * halves * rows :, :] = codes
-                b_copy(s, dy).start()
+                for d in range(GROUP):
+                    blocks = []
+                    for j in (2 * d, 2 * d + 1):
+                        for r in range(slots):
+                            for i in range(halves):
+                                at = (r, slice(j * rows, (j + 1) * rows), slice(i * LANES, (i + 1) * LANES))
+                                blocks.append(own[(s, *at)] + a_in[(s, dy, *at)])
+                    coded, codes = encode(blocks)
+                    f = (dy - 1) * GROUP + d
+                    for n, block in enumerate(coded):
+                        b_out[s, f, n * rows : (n + 1) * rows, :] = block
+                    b_out[s, f, 2 * slots * halves * rows :, :] = codes
+                    b_copy(s, dy, d).start()
             if dy == n_y - 1:
                 for t in range(1, GROUP):
                     pump((s + 1) * GROUP + t)
@@ -334,12 +356,13 @@
         for k in range(PACK):
             if s + 1 < n_u:
                 ring_copy(s, k).wait_send()
-            pair_copy(s, k).wait_send()
+            (relay_copy() if (s, k) == (turn, 1) else pair_copy(s, k)).wait_send()
     for s in range(n_g):
         for dy in range(n_y):
             a_copy(s, dy).wait_send()
             if dy:
-                b_copy(s, dy).wait_send()
+                for d in range(GROUP):
+                    b_copy(s, dy, d).wait_send()
         for j in range(blocks_g):
             if s or j:
                 c_copy(s, j).wait_send()
@@ -362,7 +385,7 @@
     vmem = pl.BlockSpec(memory_space=pltpu.VMEM)
     i16, i32 = jnp.int16, jnp.int32
     halves = cols // LANES
-    b_rows = slots * halves * wide + META
+    b_rows = 2 * slots * halves * rows + META
     units = slots * halves * (rows // META) + 1
     d_rows = out_tiles * halves * rows + META
     return pl.pallas_call(
@@ -382,8 +405,8 @@
             pltpu.VMEM((n_g, n_y, slots, wide, cols), f32),
             pltpu.VMEM((n_g, n_y, slots, wide, cols), f32),
             pltpu.VMEM((n_g, slots, wide, cols), f32),
-            pltpu.VMEM((n_g, n_y - 1, b_rows, LANES), i16),
-            pltpu.VMEM((n_g, n_y - 1, b_rows, LANES), i16),
+            pltpu.VMEM((n_g, (n_y - 1) * GROUP, b_rows, LANES), i16),
+            pltpu.VMEM((n_g, (n_y - 1) * GROUP, b_rows, LANES), i16),
             pltpu.VMEM((n_g, 2 * GROUP, units, META, LANES), i16),
             pltpu.VMEM((n_occ * units, META, LANES), i16),
             pltpu.VMEM((n_vir, d_rows, LANES), i16),
@@ -391,12 +414,12 @@
             dma((slots,)),
             dma((n_u, PACK)), dma((n_u, PACK)), dma((n_u, PACK)), dma((n_u, PACK)),
             dma((n_g, n_y)), dma((n_g, n_y)),
-            dma((n_g, n_y)), dma((n_g, n_y)),
+            dma((n_g, (n_y - 1) * GROUP)), dma((n_g, (n_y - 1) * GROUP)),
             dma((n_g, 2 * GROUP)), dma((n_occ,)),
             dma((n_vir,)), dma((n_vir,)),
         ],
         compiler_params=pltpu.CompilerParams(
-            collective_id=0, has_side_effects=True, vmem_limit_bytes=64 * 1024 * 1024
+            collective_id=0, has_side_effects=True, vmem_limit_bytes=64 * 1024 * 1024 - 4 * rows * out_tiles * entries
         ),
         cost_estimate=pl.CostEstimate(
             flops=2 * n_occ * rows * slots * tiles * entries * entries,

time: 45 us -> 43.6 us (0.969)
  Pallas kernels: 42.9 us -> 41.5 us
    pallas_call x1, Pallas kernels: 42.9 us -> 41.5 us  [shards(): pl.pallas_call(functools.partial(kernel, n_occ, n_vir), out_shape=jax.Sha...]
where the time goes in v4:
time: 43.6 us; the launch traced here: 43.4 us
  Pallas kernels  41.5 us (95%)
  local copies, waits for them, and re-layouts  1.87 us (4%)
    pallas_call x1, Pallas kernels, shards(): pl.pallas_call(functools.partial(kernel, n_occ, n_vir), out_shape=jax.Sha...  41.5 us
    unnamed x1, local copies, waits for them, and re-layouts  1.87 us

profile of v4, /device:TPU:0, one launch (start us, length us, event | category | flops | bytes accessed | tf_op | source)
XLA Modules:
  0.0 43.4 jit_solution(10821649621454533899)
XLA Ops:
  0.0 41.5 %shard_map.55 = f32[32,4096]{1,0:T(8,128)} custom-call(bf16[32,4096]{1,0:T(8,128)(2,1)} %amp_hbm.1, s32[1,4]{1,0:T(1,128)} %tile_hbm.1, s32[2,4]{1,0:T(2,128)} %block_hbm.1, s32[16]{0:T(128)} %owner_hbm.1, bf16[2,4096,1024]{2,1,0:T(8,128)(2,1)} %bitcast.1), custom_call_target="tpu_custom_call" | custom-call | flops 4294967296 | bytes 16777216 | tf_op jit(solution)/shard_map/pallas_call | solution.py:391
  41.5 1.9 %copy.7 = f32[32,4096]{1,0:T(8,128)} copy(f32[32,4096]{1,0:T(8,128)} %shard_map.55) | data formatting | bytes 1048576

commit v5 on v4

--- a/solution.py
+++ b/solution.py
@@ -9,7 +9,7 @@
 
 MESH = pl.DeviceIdType.MESH
 LANES = 128
-GROUP = 2
+GROUP = 1
 PACK = 2
 META = 16
 TOP = 32700.0
@@ -256,21 +256,21 @@
             for t in range(1, GROUP):
                 pump(t)
 
+        for d in range(GROUP):
+            for k in range(PACK):
+                pair_wait(s * GROUP + d, k)
+
+            @pl.when(s * GROUP + d == turn - 1)
+            def _():
+                relay_copy().start()
+
+            if d == GROUP - 1:
+                pump((s + 1) * GROUP)
+            spread(s, d)
+
         @pl.when(s > 0)
         def _():
             finish(s - 1)
-
-        for d in range(GROUP):
-            for k in range(PACK):
-                pair_wait(s * GROUP + d, k)
-
-            @pl.when(s * GROUP + d == turn - 1)
-            def _():
-                relay_copy().start()
-
-            if d == GROUP - 1:
-                pump((s + 1) * GROUP)
-            spread(s, d)
 
         @pl.when(s == 0)
         def _():

time: 43.6 us -> 44.9 us (1.030)
  Pallas kernels: 41.5 us -> 42.8 us
    pallas_call x1, Pallas kernels: 41.5 us -> 42.8 us  [shards(): pl.pallas_call(functools.partial(kernel, n_occ, n_vir), out_shape=jax.Sha...]
where the time goes in v5:
time: 44.9 us; the launch traced here: 44.6 us
  Pallas kernels  42.8 us (95%)
  local copies, waits for them, and re-layouts  1.87 us (4%)
    pallas_call x1, Pallas kernels, shards(): pl.pallas_call(functools.partial(kernel, n_occ, n_vir), out_shape=jax.Sha...  42.8 us
    unnamed x1, local copies, waits for them, and re-layouts  1.87 us

profile of v5, /device:TPU:0, one launch (start us, length us, event | category | flops | bytes accessed | tf_op | source)
XLA Modules:
  0.0 44.6 jit_solution(17292300374042498421)
XLA Ops:
  0.0 42.8 %shard_map.55 = f32[32,4096]{1,0:T(8,128)} custom-call(bf16[32,4096]{1,0:T(8,128)(2,1)} %amp_hbm.1, s32[1,4]{1,0:T(1,128)} %tile_hbm.1, s32[2,4]{1,0:T(2,128)} %block_hbm.1, s32[16]{0:T(128)} %owner_hbm.1, bf16[2,4096,1024]{2,1,0:T(8,128)(2,1)} %bitcast.1), custom_call_target="tpu_custom_call" | custom-call | flops 4294967296 | bytes 16777216 | tf_op jit(solution)/shard_map/pallas_call | solution.py:391
  42.8 1.9 %copy.7 = f32[32,4096]{1,0:T(8,128)} copy(f32[32,4096]{1,0:T(8,128)} %shard_map.55) | data formatting | bytes 1048576
